TPU v7x, 32 devices: a whole 2x2x4 slice. The times are simulated.
32 devices in a mesh: group: 2 (over x), lat: 16 (over z, y, core).
Axes of the slice: x: 2, y: 2, z: 4, core: 2. Of those that a mesh axis runs over, the one named last changes fastest.
Arguments:
- grad_out: bfloat16 [128, 3, 2048], P(('group', 'lat')), parts along dimension 0, may hold values from -6 to 6
- layer_inputs: bfloat16 [128, 3, 2048], P(('group', 'lat')), parts along dimension 0, may hold values from -6 to 6
- active: int32 [128, 3, 16384], P('group', None, 'lat'), parts along dimension 0, may hold values 0 or 1
- enc_weight: bfloat16 [3, 2048, 16384], P(None, None, 'lat'), may hold values from -0.046875 to 0.046875
- dec_weight: bfloat16 [6, 16384, 2048], P(None, 'lat'), may hold values from -0.125 to 0.125
Outputs:
- enc_grad: bfloat16 [6, 2048, 16384], P('group', None, 'lat'), parts along dimension 0
- input_grad: bfloat16 [128, 3, 2048], P(('group', 'lat')), parts along dimension 0
There are 2 independent parts, one for each index of `group`. A program takes and returns all parts, laid end to end along the dimension named above; an argument that names none is the same for every part. Nothing has to cross between parts.
All inputs are finite; a program needn't handle non-finite values. No bound on the sum of `active` on one device may be relied on, other than what follows from the above.
Results may differ from a plain program's by a relative error of at most 0.0049.
Values may be sent and summed in bfloat16 or wider, within the bound.
A program may use at most 128 MiB of HBM per device.

v0:
```python
import jax
import jax.numpy as jnp
from jax import lax
from jax.sharding import PartitionSpec as P


def pair_index(source, target, layers):
    return source * layers - source * (source - 1) // 2 + target - source


def per_device(grad_out, layer_inputs, active, enc_weight, dec_weight):
    layers = grad_out.shape[1]
    local_latents = enc_weight.shape[2]
    own_rows = grad_out.shape[0]
    tokens = own_rows * lax.axis_size("lat")
    piece = lax.all_gather(grad_out, "lat", axis=0, tiled=True)
    count = piece.shape[0]
    gates = active.astype(jnp.float32)
    columns = []
    for source in range(layers):
        total = jnp.zeros((count, local_latents), jnp.float32)
        for target in range(source, layers):
            weight = dec_weight[pair_index(source, target, layers)]
            total = total + lax.dot_general(
                piece[:, target, :],
                weight,
                (((1,), (1,)), ((), ())),
                preferred_element_type=jnp.float32,
            )
        columns.append((total * gates[:, source, :]).astype(jnp.bfloat16))
    pre_grad = jnp.stack(columns, axis=1)
    grads = pre_grad
    enc_total = jnp.einsum(
        "rld,rlf->ldf",
        lax.all_gather(layer_inputs, "lat", axis=0, tiled=True),
        grads,
        preferred_element_type=jnp.float32,
    )
    enc_grad = (enc_total * tokens ** (-0.5)).astype(jnp.bfloat16)
    grads = pre_grad
    summed = lax.psum_scatter(
        jnp.einsum("rlf,ldf->rld", grads, enc_weight, preferred_element_type=jnp.float32),
        "lat",
        scatter_dimension=0,
        tiled=True,
    )
    return (enc_grad, summed.astype(jnp.bfloat16))


def solution(mesh):
    return jax.shard_map(
        per_device,
        mesh=mesh,
        in_specs=(
            P(("group", "lat"), None, None),
            P(("group", "lat"), None, None),
            P("group", None, "lat"),
            P(None, None, "lat"),
            P(None, "lat", None),
        ),
        out_specs=(P("group", None, "lat"), P(("group", "lat"), None, None)),
        check_vma=False,
    )
```

profile of v0, /device:TPU:0, one launch (start us, length us, event | category | flops | bytes accessed | tf_op | source)
XLA Modules:
  0.0 178.8 jit_solution(6534827146588343581)
XLA Ops:
  0.6 1.2 dynamic-slice
  2.5 0.8 copy.12
  3.4 0.8 copy.16
  4.2 1.2 convert_element_type.21
  5.4 26.2 %all_gather.7 = bf16[64,3,2048]{2,1,0:T(4,128)(2,1)S(1)} all-gather(bf16[4,3,2048]{2,1,0:T(4,128)(2,1)S(1)} %copy.16), channel_id=1, replica_groups=mesh['group'=2,'lat'=16] {'lat'}, dimensions={0}, use_global_device_ids=true | all-gather | bytes 835584 | tf_op jit(solution)/shard_map/all_gather | solution.py:35
  31.7 20.5 %all_gather.6 = bf16[64,3,2048]{2,1,0:T(4,128)(2,1)S(1)} all-gather(bf16[4,3,2048]{2,1,0:T(4,128)(2,1)S(1)} %copy.12), channel_id=1, replica_groups=mesh['group'=2,'lat'=16] {'lat'}, dimensions={0}, use_global_device_ids=true | all-gather | bytes 835584 | tf_op jit(solution)/shard_map/all_gather | solution.py:16
  52.2 1.1 fusion.58
  53.3 3.6 %fusion.52 = bf16[64,1,1024]{2,0,1:T(8,128)(2,1)S(1)} fusion(bf16[6,1024,2048]{2,1,0:T(8,128)(2,1)} %param.9, f32[64,3,1024]{2,0,1:T(8,128)S(1)} %convert_element_type.21, bf16[64,1,2048]{2,1,0:T(2,128)(2,1)S(1)} %get-tuple-element.10), kind=kOutput, calls=%fused_computation.32 | convolution fusion | flops 268566528 | bytes 4849664 | tf_op jit(solution)/shard_map/dot_general | solution.py:24
  56.9 3.7 %fusion.9 = f32[64,1024]{1,0:T(8,128)S(1)} fusion(bf16[6,1024,2048]{2,1,0:T(8,128)(2,1)} %param.9, bf16[64,1,2048]{2,1,0:T(2,128)(2,1)S(1)} %get-tuple-element.9), kind=kOutput, calls=%fused_computation.10 | convolution fusion | flops 268435456 | bytes 4718592 | tf_op jit(solution)/shard_map/dot_general | solution.py:24
  60.6 0.0 slice-start.1
  60.6 3.7 %fusion.3 = f32[64,1024]{1,0:T(8,128)S(1)} fusion(bf16[6,1024,2048]{2,1,0:T(8,128)(2,1)} %param.9, bf16[64,1,2048]{2,1,0:T(2,128)(2,1)S(1)} %get-tuple-element.10), kind=kOutput, calls=%fused_computation.4 | convolution fusion | flops 268435456 | bytes 4718592 | tf_op jit(solution)/shard_map/dot_general | solution.py:24
  64.3 3.6 %fusion.49 = bf16[64,1,1024]{2,0,1:T(8,128)(2,1)S(1)} fusion(f32[64,1024]{1,0:T(8,128)S(1)} %fusion.3, bf16[6,1024,2048]{2,1,0:T(8,128)(2,1)} %param.9, f32[64,3,1024]{2,0,1:T(8,128)S(1)} %convert_element_type.21, bf16[64,1,2048]{2,1,0:T(2,128)(2,1)S(1)} %get-tuple-element.9), kind=kOutput, calls=%fused_computation.31 | convolution fusion | flops 268632064 | bytes 5111808 | tf_op jit(solution)/shard_map/dot_general | solution.py:24
  67.9 0.0 slice-start.2
  68.0 3.7 %fusion.7 = f32[64,1024]{1,0:T(8,128)S(1)} fusion(bf16[6,1024,2048]{2,1,0:T(8,128)(2,1)} %param.9, bf16[64,1,2048]{2,1,0:T(2,128)(2,1)S(1)} %get-tuple-element.10), kind=kOutput, calls=%fused_computation.8 | convolution fusion | flops 268435456 | bytes 4718592 | tf_op jit(solution)/shard_map/dot_general | solution.py:24
  71.7 4.2 %fusion.46 = bf16[64,1,1024]{2,0,1:T(8,128)(2,1)} fusion(f32[64,1024]{1,0:T(8,128)S(1)} %fusion.7, f32[64,1024]{1,0:T(8,128)S(1)} %fusion.9, bf16[6,1024,2048]{2,1,0:T(8,128)(2,1)} %param.9, f32[64,3,1024]{2,0,1:T(8,128)S(1)} %convert_element_type.21, bf16[64,1,2048]{2,1,0:T(2,128)(2,1)S(1)} %get-tuple-element.8), kind=kOutput, calls=%fused_computation.30 | convolution fusion | flops 268697600 | bytes 5373952 | tf_op jit(solution)/shard_map/dot_general | solution.py:24
  75.9 0.0 copy-done
  75.9 0.0 slice-done
  75.9 0.0 slice-done.1
  76.0 0.0 slice-done.2
  76.0 4.8 %convolution_bitcast_fusion = f32[64,3,2048]{2,0,1:T(8,128)S(1)} fusion(bf16[3,2048,1024]{2,1,0:T(8,128)(2,1)S(1)} %bitcast.79, bf16[64,1,1024]{2,0,1:T(8,128)(2,1)S(1)} %fusion.52, bf16[64,1,1024]{2,0,1:T(8,128)(2,1)S(1)} %fusion.49, bf16[64,1,1024]{2,0,1:T(8,128)(2,1)} %fusion.46), kind=kOutput, calls=%fused_computation.20 | convolution fusion | flops 805699584 | bytes 14548992 | tf_op jit(solution)/shard_map/rlf,ldf->rld/dot_general | solution.py:42
  80.8 73.3 %all-reduce.2 = bf16[64,3,2048]{2,0,1:T(8,128)(2,1)S(1)} all-reduce(f32[64,3,2048]{2,0,1:T(8,128)S(1)} %convolution_bitcast_fusion), channel_id=2, replica_groups=mesh['group'=2,'lat'=16] {'lat'}, use_global_device_ids=true, to_apply=%region_0.0.clone | all-reduce | flops 393216 | bytes 2359296
  154.2 0.7 dynamic-slice_convert_fusion
  154.8 7.4 %fusion = bf16[3,2048,1024]{1,2,0:T(8,128)(2,1)} fusion(bf16[64,3,2048]{2,1,0:T(4,128)(2,1)S(1)} %all_gather.7, bf16[64,1,1024]{2,0,1:T(8,128)(2,1)S(1)} %fusion.52, bf16[64,1,1024]{2,0,1:T(8,128)(2,1)} %copy-done, bf16[64,1,1024]{2,0,1:T(8,128)(2,1)} %fusion.46), kind=kOutput, calls=%fused_computation.1 | convolution fusion | flops 818282496 | bytes 13762560 | tf_op jit(solution)/shard_map/rld,rlf->ldf/dot_general | solution.py:33
  162.2 16.6 %copy.18 = bf16[3,2048,1024]{2,1,0:T(8,128)(2,1)} copy(bf16[3,2048,1024]{1,2,0:T(8,128)(2,1)} %fusion) | data formatting | bytes 25165824
  (3 shorter events, 0.0 us)
Async XLA Ops:
  56.9 19.1 %slice-start = ((s8[12582912]{0:T(1024)(128)(4,1)}), s8[4194304]{0:T(1024)(128)(4,1)S(1)}, s32[]{:S(2)}) async-start(s8[12582912]{0:T(1024)(128)(4,1)} %bitcast.78), calls=%async_computation | async-start | bytes 8388608
  60.6 15.4 %slice-start.1 = ((s8[12582912]{0:T(1024)(128)(4,1)}), s8[4194304]{0:T(1024)(128)(4,1)S(1)}, s32[]{:S(2)}) async-start(s8[12582912]{0:T(1024)(128)(4,1)} %bitcast.78), calls=%async_computation.1 | async-start | bytes 8388608
  67.9 8.0 %copy-start = (bf16[64,1,1024]{2,0,1:T(8,128)(2,1)}, bf16[64,1,1024]{2,0,1:T(8,128)(2,1)S(1)}, u32[]{:S(2)}) copy-start(bf16[64,1,1024]{2,0,1:T(8,128)(2,1)S(1)} %fusion.49) | copy-start | bytes 393220
  67.9 8.0 %slice-start.2 = ((s8[12582912]{0:T(1024)(128)(4,1)}), s8[4194304]{0:T(1024)(128)(4,1)S(1)}, s32[]{:S(2)}) async-start(s8[12582912]{0:T(1024)(128)(4,1)} %bitcast.78), calls=%async_computation.2 | async-start | bytes 8388608
where the time goes:
time: 180 us; the launch traced here: 179 us
  blocking collectives  120 us (67%)
  matrix products  34.8 us (19%)
  local copies, waits for them, and re-layouts  21.3 us (12%)
    unnamed x1, blocking collectives  73.3 us
    all_gather x1, blocking collectives, per_device(): lax.all_gather(layer_inputs, 'lat', axis=0, tiled=True)  26.2 us
    dot_general x6, matrix products, per_device(): lax.dot_general(piece[:, target, :], weight, (((1,), (1,)), ((), ())), pr...  22.6 us
    all_gather x1, blocking collectives, per_device(): piece = lax.all_gather(grad_out, 'lat', axis=0, tiled=True)  20.5 us
    unnamed x12, local copies, waits for them, and re-layouts  19.5 us
    dot_general x1, matrix products, per_device(): jnp.einsum('rld,rlf->ldf', lax.all_gather(layer_inputs, 'lat', axis=0, ti...  7.37 us
    dot_general x1, matrix products, per_device(): jnp.einsum('rlf,ldf->rld', grads, enc_weight, preferred_element_type=jnp....  4.83 us

commit v1 on v0

v1 whole, which is shorter than its diff:
```python
import functools

import jax
import jax.numpy as jnp
from jax import lax
from jax.experimental import pallas as pl
from jax.experimental.pallas import tpu as pltpu
from jax.sharding import PartitionSpec as P

MESH = pl.DeviceIdType.MESH
F32 = jnp.float32
BF16 = jnp.bfloat16
NT = (((1,), (1,)), ((), ()))
TN = (((0,), (0,)), ((), ()))


def pair_index(source, target, layers):
    return source * layers - source * (source - 1) // 2 + target - source


def natural_of(index):
    q = index >> 6
    hh = (index >> 4) & 3
    y = (index >> 3) & 1
    c = (index >> 2) & 1
    r = index & 3
    return (c * 2 + y) * 64 + hh * 16 + r * 4 + q


def exchange_kernel(
    n, layers, rows, width,
    g_ref, x_ref, act_hbm, enc_hbm, dec_hbm,
    pre_hbm, xg_hbm, ig_ref,
    act_v, enc_v, dec_v, own32, out32, mask_v, gat, nat, pre_v, stage,
    s1, r1, keep, s2, r2, s3, r3, perm, perm_t,
    w_sem, o_sem, zs, zr, ys, yr, cs, cr, s1s, s1r, s2s, s2r, s3s, s3r,
):
    high = n // 4
    groups = n // 16
    tokens = rows * n
    q_width = width // 4
    local = enc_v.shape[2]
    tile = 256
    me = lax.axis_index("lat")
    group = lax.axis_index("group")
    c = me % 2
    y = (me // 2) % 2
    h = me // 4
    l_mine = c * 2 + y
    core_peer = me + 1 - 2 * c
    y_peer = me + 2 - 4 * y
    z_peers = [((h + j) % high) * 4 + me % 4 for j in range(1, high)]

    weight = {}
    count = 0

    def load(src, dst):
        nonlocal count
        copy = pltpu.make_async_copy(src, dst, w_sem.at[count])
        copy.start()
        count += 1
        return copy

    barrier = pltpu.get_barrier_semaphore()
    for peer in z_peers + [y_peer, core_peer]:
        pl.semaphore_signal(barrier, inc=1, device_id=(group, peer), device_id_type=MESH)

    act_copy = load(act_hbm, act_v)
    for source in reversed(range(layers)):
        for target in range(source, layers):
            p = pair_index(source, target, layers)
            weight["dec", p] = load(dec_hbm.at[p], dec_v.at[p])
        weight["enc", source] = load(enc_hbm.at[source], enc_v.at[source])

    for a, ref in enumerate((g_ref, x_ref)):
        for r in range(rows):
            value = ref[r].astype(F32)
            for t in range(layers):
                for q in range(4):
                    own32[a * layers + t, pl.ds(r * 4 + q, 1), :] = value[t : t + 1, q * q_width : (q + 1) * q_width]
    for k in range(2 * layers):
        gat.at[k, l_mine, h][...] = own32[k].astype(BF16)

    pl.semaphore_wait(barrier, len(z_peers) + 2)

    def remote(src, dst, send, recv, peer):
        copy = pltpu.make_async_remote_copy(
            src_ref=src, dst_ref=dst, send_sem=send, recv_sem=recv,
            device_id=(group, peer), device_id_type=MESH,
        )
        copy.start()
        return copy

    sent = []
    z_of, y_of, c_of = {}, {}, {}

    def z_start(k):
        z_of[k] = [
            remote(gat.at[k, l_mine, h], gat.at[k, l_mine, h], zs.at[k, j], zr.at[k, j], peer)
            for j, peer in enumerate(z_peers)
        ]
        sent.extend(z_of[k])

    def y_start(k):
        for copy in z_of[k]:
            copy.wait_recv()
        y_of[k] = remote(gat.at[k, l_mine], gat.at[k, l_mine], ys.at[k], yr.at[k], y_peer)
        sent.append(y_of[k])

    def c_start(k):
        y_of[k].wait_recv()
        c_of[k] = remote(
            gat.at[k, pl.ds(c * 2, 2)], gat.at[k, pl.ds(c * 2, 2)], cs.at[k], cr.at[k], core_peer
        )
        sent.append(c_of[k])

    def gathered(k):
        c_of[k].wait_recv()
        for gi in range(groups):
            block = gat[k, :, pl.ds(gi * 4, 4)].reshape(256, q_width)
            moved = jnp.dot(perm[...], block, preferred_element_type=F32).astype(BF16)
            for q in range(4):
                nat[k, pl.ds(gi * 64, 64), pl.ds(q * q_width, q_width)] = moved[q * 64 : (q + 1) * 64]

    order = list(reversed(range(layers)))
    for t in order:
        z_start(t)

    row = lax.broadcasted_iota(jnp.int32, (256, 256), 0)
    col = lax.broadcasted_iota(jnp.int32, (256, 256), 1)
    perm[...] = jnp.where(natural_of(row) == col, 1.0, 0.0).astype(BF16)
    perm_t[...] = jnp.where(natural_of(col) == row, 1.0, 0.0).astype(BF16)
    act_copy.wait()
    for s in order:
        mask_v[s] = act_v[:, s, :].astype(F32)

    def source_grad(s):
        pairs = [pair_index(s, t, layers) for t in range(s, layers)]
        for p in pairs:
            weight["dec", p].wait()

        def body(i, carry):
            cols = pl.ds(pl.multiple_of(i * tile, tile), tile)
            total = jnp.zeros((tokens, tile), F32)
            for t, p in zip(range(s, layers), pairs):
                total = total + lax.dot_general(nat[t], dec_v[p, cols, :], NT, preferred_element_type=F32)
            pre_v[s, :, cols] = (total * mask_v[s, :, cols]).astype(BF16)
            return carry

        lax.fori_loop(0, local // tile, body, 0)

    out_copies = []

    def save(src, dst):
        copy = pltpu.make_async_copy(src, dst, o_sem.at[len(out_copies)])
        copy.start()
        out_copies.append(copy)

    first, second, third = {}, {}, {}

    def input_partial(s):
        weight["enc", s].wait()

        def body(q, carry):
            deep = pl.ds(pl.multiple_of(q * q_width, q_width), q_width)
            part = lax.dot_general(pre_v[s], enc_v[s, deep, :], NT, preferred_element_type=F32).astype(BF16)
            for gi in range(groups):
                stage[s, gi, q] = part[gi * 64 : (gi + 1) * 64]
            return carry

        lax.fori_loop(0, 4, body, 0)
        for gi in range(groups):
            block = stage[s, gi].reshape(256, q_width)
            moved = jnp.dot(perm_t[...], block, preferred_element_type=F32).astype(BF16)
            s1[s, :, pl.ds(gi * 4, 4)] = moved.reshape(4, 4, 16, q_width)
        first[s] = remote(s1.at[s, pl.ds(2 - c * 2, 2)], r1.at[s], s1s.at[s], s1r.at[s], core_peer)
        sent.append(first[s])

    def reduce_y(s):
        first[s].wait_recv()
        s2[s] = (s1[s, c * 2 + 1 - y].astype(F32) + r1[s, 1 - y].astype(F32)).astype(BF16)
        second[s] = remote(s2.at[s], r2.at[s], s2s.at[s], s2r.at[s], y_peer)
        sent.append(second[s])
        keep[s] = s1[s, l_mine].astype(F32) + r1[s, y].astype(F32)

    def reduce_z(s):
        second[s].wait_recv()
        total = keep[s] + r2[s].astype(F32)
        keep[s] = total
        s3[s] = total.astype(BF16)
        third[s] = [
            remote(s3.at[s, (h + j + 1) % high], r3.at[s, j], s3s.at[s, j], s3r.at[s, j], peer)
            for j, peer in enumerate(z_peers)
        ]
        sent.extend(third[s])

    def finish(s):
        total = keep[s, h]
        for j, copy in enumerate(third[s]):
            copy.wait_recv()
            total = total + r3[s, j].astype(F32)
        for r in range(rows):
            for q in range(4):
                out32[r, pl.ds(s, 1), pl.ds(q * q_width, q_width)] = total[r * 4 + q : r * 4 + q + 1]

    def x_ready(k):
        gathered(k)
        save(nat.at[k], xg_hbm.at[k - layers])

    hidden = []
    for t in order:
        y_start(t)
    for t in order:
        c_start(t)
        z_start(layers + t)
    for i, s in enumerate(order):
        gathered(s)
        source_grad(s)
        save(pre_v.at[s], pre_hbm.at[s])
        y_start(layers + s)
        if i >= 1:
            reduce_y(order[i - 1])
        input_partial(s)
        if i >= 1:
            reduce_z(order[i - 1])
            c_start(layers + order[i - 1])
        if i >= 2:
            finish(order[i - 2])
            x_ready(layers + order[i - 2])
    last = order[-1]
    reduce_y(last)
    c_start(layers + last)
    for s in order[:-1][-1:]:
        finish(s)
        x_ready(layers + s)
    reduce_z(last)
    x_ready(layers + last)
    finish(last)
    ig_ref[...] = out32[...].astype(BF16)
    for copy in out_copies:
        copy.wait()
    for copy in sent:
        copy.wait_send()


def outer_kernel(scale, x_ref, pre_ref, out_ref):
    out_ref[0] = (lax.dot_general(x_ref[0], pre_ref[0], TN, preferred_element_type=F32) * scale).astype(BF16)


def per_device(n, grad_out, layer_inputs, active, enc_weight, dec_weight):
    rows, layers, width = grad_out.shape
    local = enc_weight.shape[2]
    tokens = rows * n
    high = n // 4
    q_width = width // 4
    dma = pltpu.SemaphoreType.DMA
    pairs = dec_weight.shape[0]
    any_space = pl.BlockSpec(memory_space=pl.ANY)
    vmem = pl.BlockSpec(memory_space=pltpu.VMEM)
    macs = tokens * local * width * (pairs + layers)
    pre, xg, input_grad = pl.pallas_call(
        functools.partial(exchange_kernel, n, layers, rows, width),
        out_shape=(
            jax.ShapeDtypeStruct((layers, tokens, local), BF16),
            jax.ShapeDtypeStruct((layers, tokens, width), BF16),
            jax.ShapeDtypeStruct((rows, layers, width), BF16),
        ),
        in_specs=[vmem, vmem, any_space, any_space, any_space],
        out_specs=(any_space, any_space, vmem),
        scratch_shapes=[
            pltpu.VMEM((tokens, layers, local), jnp.int32),
            pltpu.VMEM((layers, width, local), BF16),
            pltpu.VMEM((pairs, local, width), BF16),
            pltpu.VMEM((2 * layers, 16, q_width), F32),
            pltpu.VMEM((rows, layers, width), F32),
            pltpu.VMEM((layers, tokens, local), F32),
            pltpu.VMEM((2 * layers, 4, high, 16, q_width), BF16),
            pltpu.VMEM((2 * layers, tokens, width), BF16),
            pltpu.VMEM((layers, tokens, local), BF16),
            pltpu.VMEM((layers, n // 16, 4, 64, q_width), BF16),
            pltpu.VMEM((layers, 4, high, 16, q_width), BF16),
            pltpu.VMEM((layers, 2, high, 16, q_width), BF16),
            pltpu.VMEM((layers, high, 16, q_width), F32),
            pltpu.VMEM((layers, high, 16, q_width), BF16),
            pltpu.VMEM((layers, high, 16, q_width), BF16),
            pltpu.VMEM((layers, high, 16, q_width), BF16),
            pltpu.VMEM((layers, high - 1, 16, q_width), BF16),
            pltpu.VMEM((256, 256), BF16),
            pltpu.VMEM((256, 256), BF16),
            dma((1 + pairs + layers,)),
            dma((2 * layers,)),
            dma((2 * layers, high - 1)),
            dma((2 * layers, high - 1)),
            dma((2 * layers,)),
            dma((2 * layers,)),
            dma((2 * layers,)),
            dma((2 * layers,)),
            dma((layers,)),
            dma((layers,)),
            dma((layers,)),
            dma((layers,)),
            dma((layers, high - 1)),
            dma((layers, high - 1)),
        ],
        compiler_params=pltpu.CompilerParams(
            collective_id=0, has_side_effects=True, vmem_limit_bytes=60 * 1024 * 1024
        ),
        cost_estimate=pl.CostEstimate(
            flops=2 * macs,
            bytes_accessed=2 * local * width * (pairs + layers),
            transcendentals=0,
        ),
    )(grad_out, layer_inputs, active, enc_weight, dec_weight)

    deep = 512
    enc_grad = pl.pallas_call(
        functools.partial(outer_kernel, tokens ** (-0.5)),
        grid=(layers, width // deep),
        in_specs=[
            pl.BlockSpec((1, tokens, deep), lambda l, d: (l, 0, d)),
            pl.BlockSpec((1, tokens, local), lambda l, d: (l, 0, 0)),
        ],
        out_specs=pl.BlockSpec((1, deep, local), lambda l, d: (l, d, 0)),
        out_shape=jax.ShapeDtypeStruct((layers, width, local), BF16),
        compiler_params=pltpu.CompilerParams(vmem_limit_bytes=32 * 1024 * 1024),
        cost_estimate=pl.CostEstimate(
            flops=2 * tokens * local * width * layers,
            bytes_accessed=2 * local * width * layers,
            transcendentals=0,
        ),
    )(xg, pre)
    return enc_grad, input_grad


def solution(mesh):
    return jax.shard_map(
        functools.partial(per_device, mesh.shape["lat"]),
        mesh=mesh,
        in_specs=(
            P(("group", "lat"), None, None),
            P(("group", "lat"), None, None),
            P("group", None, "lat"),
            P(None, None, "lat"),
            P(None, "lat", None),
        ),
        out_specs=(P("group", None, "lat"), P(("group", "lat"), None, None)),
        check_vma=False,
    )
```

time: 180 us -> 64.5 us (0.36)
  blocking collectives: 120 us -> 0 us
  Pallas kernels: 0 us -> 54.2 us
  matrix products: 34.8 us -> 0 us
  local copies, waits for them, and re-layouts: 21.3 us -> 9.21 us
    unnamed x1 -> x0, blocking collectives: 73.3 us -> none
    pallas_call x0 -> x2, Pallas kernels: none -> 54.2 us  [the longest x1 45.1 us: per_device(): pl.pallas_call(functools.partial(exchange_kernel, n, layers, rows, width)...]
    all_gather x2 -> x0, blocking collectives: 46.7 us -> none  [the longest x1 26.2 us: per_device(): lax.all_gather(layer_inputs, 'lat', axis=0, tiled=True)]
    dot_general x8 -> x0, matrix products: 34.8 us -> none  [the longest x6 22.6 us: per_device(): lax.dot_general(piece[:, target, :], weight, (((1,), (1,)), ((), ())), pr...]
    unnamed x12 -> x8, local copies, waits for them, and re-layouts: 19.5 us -> 9.21 us
where the time goes in v1:
time: 64.5 us; the launch traced here: 64.1 us
  Pallas kernels  54.2 us (84%)
  local copies, waits for them, and re-layouts  9.21 us (14%)
    pallas_call x1, Pallas kernels, per_device(): pl.pallas_call(functools.partial(exchange_kernel, n, layers, rows, width)...  45.1 us
    unnamed x8, local copies, waits for them, and re-layouts  9.21 us
    pallas_call x1, Pallas kernels, per_device(): pl.pallas_call(functools.partial(outer_kernel, tokens ** (-0.5)), grid=(l...  9.07 us

profile of v1, /device:TPU:0, one launch (start us, length us, event | category | flops | bytes accessed | tf_op | source)
XLA Modules:
  0.0 64.1 jit_solution(11240305291005534890)
XLA Ops:
  0.6 1.5 %copy.7.g_ref = bf16[4,3,2048]{2,1,0:T(4,128)(2,1)} copy(bf16[4,3,2048]{2,0,1:T(4,128)(2,1)} %param.5) | data formatting | bytes 98304 | tf_op args[0]
  2.1 1.5 %copy.8.x_ref = bf16[4,3,2048]{2,1,0:T(4,128)(2,1)} copy(bf16[4,3,2048]{2,0,1:T(4,128)(2,1)} %param.6) | data formatting | bytes 98304 | tf_op args[1]
  3.6 2.6 %copy.9.act_hbm = s32[64,3,1024]{2,1,0:T(4,128)} copy(s32[64,3,1024]{2,0,1:T(8,128)} %param.7) | data formatting | bytes 1572864 | tf_op args[2]
  6.2 45.1 %shard_map.68 = (bf16[3,64,1024]{2,1,0:T(8,128)(2,1)}, bf16[3,64,2048]{2,1,0:T(8,128)(2,1)}, bf16[4,3,2048]{2,1,0:T(4,128)(2,1)}) custom-call(bf16[4,3,2048]{2,1,0:T(4,128)(2,1)} %copy.7.g_ref, bf16[4,3,2048]{2,1,0:T(4,128)(2,1)} %copy.8.x_ref, s32[64,3,1024]{2,1,0:T(4,128)} %copy.9.act_hbm, bf16[3,2048,1024]{2,1,0:T(8,128)(2,1)} %enc_hbm.1, ...), custom_call_target="tpu_custom_call" | custom-call | flops 2415919104 | bytes 37748736 | tf_op jit(solution)/shard_map/pallas_call | solution.py:261
  51.4 1.5 %copy.10 = bf16[4,3,2048]{2,0,1:T(4,128)(2,1)} copy(bf16[4,3,2048]{2,1,0:T(4,128)(2,1)} %get-tuple-element.9) | data formatting | bytes 98304
  52.9 0.0 copy-start
  52.9 1.1 %copy-done = bf16[3,64,2048]{2,1,0:T(8,128)(2,1)S(1)} copy-done((bf16[3,64,2048]{2,1,0:T(8,128)(2,1)S(1)}, bf16[3,64,2048]{2,1,0:T(8,128)(2,1)}, u32[]{:S(2)}) %copy-start) | copy-done | bytes 786456
  54.0 0.0 copy-start.1
  54.0 1.0 %copy-done.1 = bf16[3,64,1024]{2,1,0:T(8,128)(2,1)S(1)} copy-done((bf16[3,64,1024]{2,1,0:T(8,128)(2,1)S(1)}, bf16[3,64,1024]{2,1,0:T(8,128)(2,1)}, u32[]{:S(2)}) %copy-start.1) | copy-done | bytes 393240
  55.0 9.1 %shard_map.69 = bf16[3,2048,1024]{2,1,0:T(8,128)(2,1)} custom-call(bf16[3,64,2048]{2,1,0:T(8,128)(2,1)S(1)} %copy-done, bf16[3,64,1024]{2,1,0:T(8,128)(2,1)S(1)} %copy-done.1), custom_call_target="tpu_custom_call" | custom-call | flops 805306368 | bytes 12582912 | tf_op jit(solution)/shard_map/pallas_call | solution.py:316
Async XLA Ops:
  52.9 1.1 %copy-start = (bf16[3,64,2048]{2,1,0:T(8,128)(2,1)S(1)}, bf16[3,64,2048]{2,1,0:T(8,128)(2,1)}, u32[]{:S(2)}) copy-start(bf16[3,64,2048]{2,1,0:T(8,128)(2,1)} %get-tuple-element.5.x_ref) | copy-start | bytes 2359300
  54.0 1.0 %copy-start.1 = (bf16[3,64,1024]{2,1,0:T(8,128)(2,1)S(1)}, bf16[3,64,1024]{2,1,0:T(8,128)(2,1)}, u32[]{:S(2)}) copy-start(bf16[3,64,1024]{2,1,0:T(8,128)(2,1)} %get-tuple-element.6.pre_ref) | copy-start | bytes 1179652

commit v2 on v1

--- a/solution.py
+++ b/solution.py
@@ -24,14 +24,14 @@
     y = (index >> 3) & 1
     c = (index >> 2) & 1
     r = index & 3
-    return (c * 2 + y) * 64 + hh * 16 + r * 4 + q
+    return (c * 2 + y) * 64 + hh * 16 + q * 4 + r
 
 
 def exchange_kernel(
     n, layers, rows, width,
     g_ref, x_ref, act_hbm, enc_hbm, dec_hbm,
     pre_hbm, xg_hbm, ig_ref,
-    act_v, enc_v, dec_v, own32, out32, mask_v, gat, nat, pre_v, stage,
+    act_v, enc_v, dec_v, own32, gat, nat, pre_v, stage,
     s1, r1, keep, s2, r2, s3, r3, perm, perm_t,
     w_sem, o_sem, zs, zr, ys, yr, cs, cr, s1s, s1r, s2s, s2r, s3s, s3r,
 ):
@@ -40,7 +40,7 @@
     tokens = rows * n
     q_width = width // 4
     local = enc_v.shape[2]
-    tile = 256
+    tile = min(512, local)
     me = lax.axis_index("lat")
     group = lax.axis_index("group")
     c = me % 2
@@ -73,11 +73,10 @@
         weight["enc", source] = load(enc_hbm.at[source], enc_v.at[source])
 
     for a, ref in enumerate((g_ref, x_ref)):
-        for r in range(rows):
-            value = ref[r].astype(F32)
-            for t in range(layers):
-                for q in range(4):
-                    own32[a * layers + t, pl.ds(r * 4 + q, 1), :] = value[t : t + 1, q * q_width : (q + 1) * q_width]
+        for t in range(layers):
+            value = ref[t].astype(F32)
+            for q in range(4):
+                own32[a * layers + t, pl.ds(q * rows, rows), :] = value[:, q * q_width : (q + 1) * q_width]
     for k in range(2 * layers):
         gat.at[k, l_mine, h][...] = own32[k].astype(BF16)
 
@@ -131,8 +130,6 @@
     perm[...] = jnp.where(natural_of(row) == col, 1.0, 0.0).astype(BF16)
     perm_t[...] = jnp.where(natural_of(col) == row, 1.0, 0.0).astype(BF16)
     act_copy.wait()
-    for s in order:
-        mask_v[s] = act_v[:, s, :].astype(F32)
 
     def source_grad(s):
         pairs = [pair_index(s, t, layers) for t in range(s, layers)]
@@ -144,7 +141,7 @@
             total = jnp.zeros((tokens, tile), F32)
             for t, p in zip(range(s, layers), pairs):
                 total = total + lax.dot_general(nat[t], dec_v[p, cols, :], NT, preferred_element_type=F32)
-            pre_v[s, :, cols] = (total * mask_v[s, :, cols]).astype(BF16)
+            pre_v[s, :, cols] = (total * act_v[s, :, cols].astype(F32)).astype(BF16)
             return carry
 
         lax.fori_loop(0, local // tile, body, 0)
@@ -199,44 +196,54 @@
         for j, copy in enumerate(third[s]):
             copy.wait_recv()
             total = total + r3[s, j].astype(F32)
-        for r in range(rows):
-            for q in range(4):
-                out32[r, pl.ds(s, 1), pl.ds(q * q_width, q_width)] = total[r * 4 + q : r * 4 + q + 1]
+        for q in range(4):
+            ig_ref[s, :, pl.ds(q * q_width, q_width)] = total[q * rows : (q + 1) * rows].astype(BF16)
 
     def x_ready(k):
         gathered(k)
         save(nat.at[k], xg_hbm.at[k - layers])
 
-    hidden = []
     for t in order:
         y_start(t)
     for t in order:
+        z_start(layers + t)
+    for t in order:
         c_start(t)
-        z_start(layers + t)
+    extra = {"y": 0, "c": 0}
+
+    def x_step(kind, many):
+        for _ in range(many):
+            if extra[kind] < layers:
+                (y_start if kind == "y" else c_start)(layers + order[extra[kind]])
+                extra[kind] += 1
+
     for i, s in enumerate(order):
+        last = i == layers - 1
         gathered(s)
+        if last:
+            x_step("y", layers)
         source_grad(s)
         save(pre_v.at[s], pre_hbm.at[s])
-        y_start(layers + s)
+        if i >= 2:
+            reduce_z(order[i - 2])
         if i >= 1:
             reduce_y(order[i - 1])
+            x_step("y", 1)
+        if last:
+            x_step("c", 1)
         input_partial(s)
-        if i >= 1:
-            reduce_z(order[i - 1])
-            c_start(layers + order[i - 1])
-        if i >= 2:
-            finish(order[i - 2])
-            x_ready(layers + order[i - 2])
-    last = order[-1]
-    reduce_y(last)
-    c_start(layers + last)
-    for s in order[:-1][-1:]:
-        finish(s)
-        x_ready(layers + s)
-    reduce_z(last)
-    x_ready(layers + last)
-    finish(last)
-    ig_ref[...] = out32[...].astype(BF16)
+    s = order[-1]
+    x_step("c", 1)
+    reduce_y(s)
+    x_step("c", layers)
+    if layers >= 2:
+        reduce_z(order[-2])
+    for t in order[:-1]:
+        x_ready(layers + t)
+    reduce_z(s)
+    x_ready(layers + s)
+    for t in order:
+        finish(t)
     for copy in out_copies:
         copy.wait()
     for copy in sent:
@@ -263,17 +270,15 @@
         out_shape=(
             jax.ShapeDtypeStruct((layers, tokens, local), BF16),
             jax.ShapeDtypeStruct((layers, tokens, width), BF16),
-            jax.ShapeDtypeStruct((rows, layers, width), BF16),
+            jax.ShapeDtypeStruct((layers, rows, width), BF16),
         ),
         in_specs=[vmem, vmem, any_space, any_space, any_space],
         out_specs=(any_space, any_space, vmem),
         scratch_shapes=[
-            pltpu.VMEM((tokens, layers, local), jnp.int32),
+            pltpu.VMEM((layers, tokens, local), jnp.int32),
             pltpu.VMEM((layers, width, local), BF16),
             pltpu.VMEM((pairs, local, width), BF16),
             pltpu.VMEM((2 * layers, 16, q_width), F32),
-            pltpu.VMEM((rows, layers, width), F32),
-            pltpu.VMEM((layers, tokens, local), F32),
             pltpu.VMEM((2 * layers, 4, high, 16, q_width), BF16),
             pltpu.VMEM((2 * layers, tokens, width), BF16),
             pltpu.VMEM((layers, tokens, local), BF16),
@@ -310,9 +315,15 @@
             bytes_accessed=2 * local * width * (pairs + layers),
             transcendentals=0,
         ),
-    )(grad_out, layer_inputs, active, enc_weight, dec_weight)
-
-    deep = 512
+    )(
+        grad_out.transpose(1, 0, 2),
+        layer_inputs.transpose(1, 0, 2),
+        active.transpose(1, 0, 2),
+        enc_weight,
+        dec_weight,
+    )
+
+    deep = width // 2
     enc_grad = pl.pallas_call(
         functools.partial(outer_kernel, tokens ** (-0.5)),
         grid=(layers, width // deep),
@@ -322,14 +333,14 @@
         ],
         out_specs=pl.BlockSpec((1, deep, local), lambda l, d: (l, d, 0)),
         out_shape=jax.ShapeDtypeStruct((layers, width, local), BF16),
-        compiler_params=pltpu.CompilerParams(vmem_limit_bytes=32 * 1024 * 1024),
+        compiler_params=pltpu.CompilerParams(vmem_limit_bytes=60 * 1024 * 1024),
         cost_estimate=pl.CostEstimate(
             flops=2 * tokens * local * width * layers,
             bytes_accessed=2 * local * width * layers,
             transcendentals=0,
         ),
     )(xg, pre)
-    return enc_grad, input_grad
+    return enc_grad, input_grad.transpose(1, 0, 2)
 
 
 def solution(mesh):

time: 64.5 us -> 49.9 us (0.77)
  local copies, waits for them, and re-layouts: 9.21 us -> 0.62 us
  Pallas kernels: 54.2 us -> 48.3 us
    unnamed x8 -> x3, local copies, waits for them, and re-layouts: 9.21 us -> 0.62 us
    pallas_call x1, Pallas kernels: 45.1 us -> 40.1 us  [per_device(): pl.pallas_call(functools.partial(exchange_kernel, n, layers, rows, width)...]
    pallas_call x1, Pallas kernels: 9.07 us -> 8.21 us  [per_device(): pl.pallas_call(functools.partial(outer_kernel, tokens ** (-0.5)), grid=(l...]
where the time goes in v2:
time: 49.9 us; the launch traced here: 49.6 us
  Pallas kernels  48.3 us (97%)
  between operations  0.65 us (1%)
  local copies, waits for them, and re-layouts  0.62 us (1%)
    pallas_call x1, Pallas kernels, per_device(): pl.pallas_call(functools.partial(exchange_kernel, n, layers, rows, width)...  40.1 us
    pallas_call x1, Pallas kernels, per_device(): pl.pallas_call(functools.partial(outer_kernel, tokens ** (-0.5)), grid=(l...  8.21 us

profile of v2, /device:TPU:0, one launch (start us, length us, event | category | flops | bytes accessed | tf_op | source)
XLA Modules:
  0.0 49.6 jit_solution(11490464306285978687)
XLA Ops:
  0.6 40.1 %shard_map.68 = (bf16[3,64,1024]{2,1,0:T(8,128)(2,1)}, bf16[3,64,2048]{2,1,0:T(8,128)(2,1)}, bf16[3,4,2048]{2,1,0:T(4,128)(2,1)}) custom-call(bf16[3,4,2048]{2,1,0:T(4,128)(2,1)} %bitcast.6, bf16[3,4,2048]{2,1,0:T(4,128)(2,1)} %bitcast.7, s32[3,64,1024]{2,1,0:T(8,128)} %bitcast.4, bf16[3,2048,1024]{2,1,0:T(8,128)(2,1)} %enc_hbm.1, bf16[6,1024,2048]{2,1,0:T(8,128)(2,1)} %dec_hbm.1), custom_call_target="tpu_custom_call" | custom-call | flops 2415919104 | bytes 37748736 | tf_op jit(solution)/shard_map/pallas_call | solution.py:268
  40.8 0.0 copy-start
  40.8 8.2 %shard_map.69 = bf16[3,2048,1024]{2,1,0:T(8,128)(2,1)} custom-call(bf16[3,64,2048]{2,1,0:T(8,128)(2,1)} %get-tuple-element.5.x_ref, bf16[3,64,1024]{2,1,0:T(8,128)(2,1)} %get-tuple-element.6.pre_ref), custom_call_target="tpu_custom_call" | custom-call | flops 805306368 | bytes 12582912 | tf_op jit(solution)/shard_map/pallas_call | solution.py:327
  49.0 0.0 copy-done
  49.0 0.6 %copy.8 = bf16[4,3,2048]{2,0,1:T(4,128)(2,1)} copy(bf16[4,3,2048]{2,0,1:T(4,128)(2,1)S(1)} %bitcast.5) | data formatting | bytes 98304
Async XLA Ops:
  40.8 8.2 %copy-start = (bf16[3,4,2048]{2,1,0:T(4,128)(2,1)S(1)}, bf16[3,4,2048]{2,1,0:T(4,128)(2,1)}, u32[]{:S(2)}) copy-start(bf16[3,4,2048]{2,1,0:T(4,128)(2,1)} %get-tuple-element.7) | copy-start | bytes 147460

commit v3 on v2

--- a/solution.py
+++ b/solution.py
@@ -32,8 +32,8 @@
     g_ref, x_ref, act_hbm, enc_hbm, dec_hbm,
     pre_hbm, xg_hbm, ig_ref,
     act_v, enc_v, dec_v, own32, gat, nat, pre_v, stage,
-    s1, r1, keep, s2, r2, s3, r3, perm, perm_t,
-    w_sem, o_sem, zs, zr, ys, yr, cs, cr, s1s, s1r, s2s, s2r, s3s, s3r,
+    s1, r1, keep, s2, r2, perm, perm_t,
+    w_sem, o_sem, zs, zr, ys, yr, cs, cr, s1s, s1r, s2s, s2r,
 ):
     high = n // 4
     groups = n // 16
@@ -49,6 +49,8 @@
     l_mine = c * 2 + y
     core_peer = me + 1 - 2 * c
     y_peer = me + 2 - 4 * y
+    chip = me // 2
+    chips = [(chip + m) % (2 * high) for m in range(1, 2 * high)]
     z_peers = [((h + j) % high) * 4 + me % 4 for j in range(1, high)]
 
     weight = {}
@@ -62,7 +64,7 @@
         return copy
 
     barrier = pltpu.get_barrier_semaphore()
-    for peer in z_peers + [y_peer, core_peer]:
+    for peer in [w * 2 + c for w in chips] + [core_peer]:
         pl.semaphore_signal(barrier, inc=1, device_id=(group, peer), device_id_type=MESH)
 
     act_copy = load(act_hbm, act_v)
@@ -80,7 +82,7 @@
     for k in range(2 * layers):
         gat.at[k, l_mine, h][...] = own32[k].astype(BF16)
 
-    pl.semaphore_wait(barrier, len(z_peers) + 2)
+    pl.semaphore_wait(barrier, len(chips) + 1)
 
     def remote(src, dst, send, recv, peer):
         copy = pltpu.make_async_remote_copy(
@@ -153,7 +155,7 @@
         copy.start()
         out_copies.append(copy)
 
-    first, second, third = {}, {}, {}
+    first, second = {}, {}
 
     def input_partial(s):
         weight["enc", s].wait()
@@ -173,29 +175,21 @@
         first[s] = remote(s1.at[s, pl.ds(2 - c * 2, 2)], r1.at[s], s1s.at[s], s1r.at[s], core_peer)
         sent.append(first[s])
 
-    def reduce_y(s):
+    def reduce_chip(s):
         first[s].wait_recv()
-        s2[s] = (s1[s, c * 2 + 1 - y].astype(F32) + r1[s, 1 - y].astype(F32)).astype(BF16)
-        second[s] = remote(s2.at[s], r2.at[s], s2s.at[s], s2r.at[s], y_peer)
-        sent.append(second[s])
-        keep[s] = s1[s, l_mine].astype(F32) + r1[s, y].astype(F32)
-
-    def reduce_z(s):
-        second[s].wait_recv()
-        total = keep[s] + r2[s].astype(F32)
-        keep[s] = total
-        s3[s] = total.astype(BF16)
-        third[s] = [
-            remote(s3.at[s, (h + j + 1) % high], r3.at[s, j], s3s.at[s, j], s3r.at[s, j], peer)
-            for j, peer in enumerate(z_peers)
+        s2[s] = (s1[s, pl.ds(c * 2, 2)].astype(F32) + r1[s].astype(F32)).astype(BF16)
+        second[s] = [
+            remote(s2.at[s, w % 2, w // 2], r2.at[s, m], s2s.at[s, m], s2r.at[s, m], w * 2 + c)
+            for m, w in enumerate(chips)
         ]
-        sent.extend(third[s])
+        sent.extend(second[s])
+        keep[s] = s1[s, l_mine, h].astype(F32) + r1[s, y, h].astype(F32)
 
     def finish(s):
-        total = keep[s, h]
-        for j, copy in enumerate(third[s]):
+        total = keep[s]
+        for m, copy in enumerate(second[s]):
             copy.wait_recv()
-            total = total + r3[s, j].astype(F32)
+            total = total + r2[s, m].astype(F32)
         for q in range(4):
             ig_ref[s, :, pl.ds(q * q_width, q_width)] = total[q * rows : (q + 1) * rows].astype(BF16)
 
@@ -224,24 +218,18 @@
             x_step("y", layers)
         source_grad(s)
         save(pre_v.at[s], pre_hbm.at[s])
-        if i >= 2:
-            reduce_z(order[i - 2])
         if i >= 1:
-            reduce_y(order[i - 1])
+            reduce_chip(order[i - 1])
             x_step("y", 1)
         if last:
             x_step("c", 1)
         input_partial(s)
     s = order[-1]
     x_step("c", 1)
-    reduce_y(s)
+    reduce_chip(s)
     x_step("c", layers)
-    if layers >= 2:
-        reduce_z(order[-2])
-    for t in order[:-1]:
+    for t in order:
         x_ready(layers + t)
-    reduce_z(s)
-    x_ready(layers + s)
     for t in order:
         finish(t)
     for copy in out_copies:
@@ -250,8 +238,20 @@
         copy.wait_send()
 
 
-def outer_kernel(scale, x_ref, pre_ref, out_ref):
-    out_ref[0] = (lax.dot_general(x_ref[0], pre_ref[0], TN, preferred_element_type=F32) * scale).astype(BF16)
+def outer_kernel(scale, x_ref, pre_ref, out_hbm, out_v, sem):
+    layers, width = out_v.shape[:2]
+    deep = width // 2
+    copies = []
+    for l in range(layers):
+        for d in range(0, width, deep):
+            rows = pl.ds(d, deep)
+            total = lax.dot_general(x_ref[l, :, rows], pre_ref[l], TN, preferred_element_type=F32)
+            out_v[l, rows, :] = (total * scale).astype(BF16)
+            copy = pltpu.make_async_copy(out_v.at[l, rows], out_hbm.at[l, rows], sem.at[len(copies)])
+            copy.start()
+            copies.append(copy)
+    for copy in copies:
+        copy.wait()
 
 
 def per_device(n, grad_out, layer_inputs, active, enc_weight, dec_weight):
@@ -285,11 +285,9 @@
             pltpu.VMEM((layers, n // 16, 4, 64, q_width), BF16),
             pltpu.VMEM((layers, 4, high, 16, q_width), BF16),
             pltpu.VMEM((layers, 2, high, 16, q_width), BF16),
-            pltpu.VMEM((layers, high, 16, q_width), F32),
-            pltpu.VMEM((layers, high, 16, q_width), BF16),
-            pltpu.VMEM((layers, high, 16, q_width), BF16),
-            pltpu.VMEM((layers, high, 16, q_width), BF16),
-            pltpu.VMEM((layers, high - 1, 16, q_width), BF16),
+            pltpu.VMEM((layers, 16, q_width), F32),
+            pltpu.VMEM((layers, 2, high, 16, q_width), BF16),
+            pltpu.VMEM((layers, 2 * high - 1, 16, q_width), BF16),
             pltpu.VMEM((256, 256), BF16),
             pltpu.VMEM((256, 256), BF16),
             dma((1 + pairs + layers,)),
@@ -302,10 +300,8 @@
             dma((2 * layers,)),
             dma((layers,)),
             dma((layers,)),
-            dma((layers,)),
-            dma((layers,)),
-            dma((layers, high - 1)),
-            dma((layers, high - 1)),
+            dma((layers, 2 * high - 1)),
+            dma((layers, 2 * high - 1)),
         ],
         compiler_params=pltpu.CompilerParams(
             collective_id=0, has_side_effects=True, vmem_limit_bytes=60 * 1024 * 1024
@@ -323,15 +319,11 @@
         dec_weight,
     )
 
-    deep = width // 2
     enc_grad = pl.pallas_call(
         functools.partial(outer_kernel, tokens ** (-0.5)),
-        grid=(layers, width // deep),
-        in_specs=[
-            pl.BlockSpec((1, tokens, deep), lambda l, d: (l, 0, d)),
-            pl.BlockSpec((1, tokens, local), lambda l, d: (l, 0, 0)),
-        ],
-        out_specs=pl.BlockSpec((1, deep, local), lambda l, d: (l, d, 0)),
+        in_specs=[vmem, vmem],
+        out_specs=any_space,
+        scratch_shapes=[pltpu.VMEM((layers, width, local), BF16), dma((2 * layers,))],
         out_shape=jax.ShapeDtypeStruct((layers, width, local), BF16),
         compiler_params=pltpu.CompilerParams(vmem_limit_bytes=60 * 1024 * 1024),
         cost_estimate=pl.CostEstimate(

time: 49.9 us -> 46.4 us (0.930)
  Pallas kernels: 48.3 us -> 44.9 us
    pallas_call x1, Pallas kernels: 40.1 us -> 38.3 us  [per_device(): pl.pallas_call(functools.partial(exchange_kernel, n, layers, rows, width)...]
    pallas_call x1, Pallas kernels: 8.21 us -> 6.62 us  [per_device(): pl.pallas_call(functools.partial(outer_kernel, tokens ** (-0.5)), in_spec...]
where the time goes in v3:
time: 46.4 us; the launch traced here: 46.2 us
  Pallas kernels  44.9 us (97%)
  between operations  0.66 us (1%)
  local copies, waits for them, and re-layouts  0.63 us (1%)
    pallas_call x1, Pallas kernels, per_device(): pl.pallas_call(functools.partial(exchange_kernel, n, layers, rows, width)...  38.3 us
    pallas_call x1, Pallas kernels, per_device(): pl.pallas_call(functools.partial(outer_kernel, tokens ** (-0.5)), in_spec...  6.62 us

profile of v3, /device:TPU:0, one launch (start us, length us, event | category | flops | bytes accessed | tf_op | source)
XLA Modules:
  0.0 46.2 jit_solution(9265038707956812126)
XLA Ops:
  0.6 38.3 %shard_map.68 = (bf16[3,64,1024]{2,1,0:T(8,128)(2,1)}, bf16[3,64,2048]{2,1,0:T(8,128)(2,1)}, bf16[3,4,2048]{2,1,0:T(4,128)(2,1)}) custom-call(bf16[3,4,2048]{2,1,0:T(4,128)(2,1)} %bitcast.6, bf16[3,4,2048]{2,1,0:T(4,128)(2,1)} %bitcast.7, s32[3,64,1024]{2,1,0:T(8,128)} %bitcast.4, bf16[3,2048,1024]{2,1,0:T(8,128)(2,1)} %enc_hbm.1, bf16[6,1024,2048]{2,1,0:T(8,128)(2,1)} %dec_hbm.1), custom_call_target="tpu_custom_call" | custom-call | flops 2415919104 | bytes 37748736 | tf_op jit(solution)/shard_map/pallas_call | solution.py:268
  38.9 0.0 copy-start
  38.9 6.6 %shard_map.69 = bf16[3,2048,1024]{2,1,0:T(8,128)(2,1)} custom-call(bf16[3,64,2048]{2,1,0:T(8,128)(2,1)} %get-tuple-element.5.x_ref, bf16[3,64,1024]{2,1,0:T(8,128)(2,1)} %get-tuple-element.6.pre_ref), custom_call_target="tpu_custom_call" | custom-call | flops 805306368 | bytes 12582912 | tf_op jit(solution)/shard_map/pallas_call | solution.py:322
  45.6 0.0 copy-done
  45.6 0.6 %copy.8 = bf16[4,3,2048]{2,0,1:T(4,128)(2,1)} copy(bf16[4,3,2048]{2,0,1:T(4,128)(2,1)S(1)} %bitcast.5) | data formatting | bytes 98304
Async XLA Ops:
  38.9 6.6 %copy-start = (bf16[3,4,2048]{2,1,0:T(4,128)(2,1)S(1)}, bf16[3,4,2048]{2,1,0:T(4,128)(2,1)}, u32[]{:S(2)}) copy-start(bf16[3,4,2048]{2,1,0:T(4,128)(2,1)} %get-tuple-element.7) | copy-start | bytes 147460

commit v4 on v3

--- a/solution.py
+++ b/solution.py
@@ -93,11 +93,16 @@
         return copy
 
     sent = []
+    second_unit = layers
+
+    def unit(k):
+        return pl.ds(k, layers if k == second_unit else 1)
+
     z_of, y_of, c_of = {}, {}, {}
 
     def z_start(k):
         z_of[k] = [
-            remote(gat.at[k, l_mine, h], gat.at[k, l_mine, h], zs.at[k, j], zr.at[k, j], peer)
+            remote(gat.at[unit(k), l_mine, h], gat.at[unit(k), l_mine, h], zs.at[k, j], zr.at[k, j], peer)
             for j, peer in enumerate(z_peers)
         ]
         sent.extend(z_of[k])
@@ -105,18 +110,19 @@
     def y_start(k):
         for copy in z_of[k]:
             copy.wait_recv()
-        y_of[k] = remote(gat.at[k, l_mine], gat.at[k, l_mine], ys.at[k], yr.at[k], y_peer)
+        y_of[k] = remote(gat.at[unit(k), l_mine], gat.at[unit(k), l_mine], ys.at[k], yr.at[k], y_peer)
         sent.append(y_of[k])
 
     def c_start(k):
         y_of[k].wait_recv()
         c_of[k] = remote(
-            gat.at[k, pl.ds(c * 2, 2)], gat.at[k, pl.ds(c * 2, 2)], cs.at[k], cr.at[k], core_peer
+            gat.at[unit(k), pl.ds(c * 2, 2)], gat.at[unit(k), pl.ds(c * 2, 2)], cs.at[k], cr.at[k], core_peer
         )
         sent.append(c_of[k])
 
     def gathered(k):
-        c_of[k].wait_recv()
+        if k in c_of:
+            c_of[k].wait_recv()
         for gi in range(groups):
             block = gat[k, :, pl.ds(gi * 4, 4)].reshape(256, q_width)
             moved = jnp.dot(perm[...], block, preferred_element_type=F32).astype(BF16)
@@ -199,42 +205,32 @@
 
     for t in order:
         y_start(t)
-    for t in order:
-        z_start(layers + t)
+    z_start(second_unit)
     for t in order:
         c_start(t)
-    extra = {"y": 0, "c": 0}
-
-    def x_step(kind, many):
-        for _ in range(many):
-            if extra[kind] < layers:
-                (y_start if kind == "y" else c_start)(layers + order[extra[kind]])
-                extra[kind] += 1
-
     for i, s in enumerate(order):
         last = i == layers - 1
         gathered(s)
         if last:
-            x_step("y", layers)
+            y_start(second_unit)
         source_grad(s)
         save(pre_v.at[s], pre_hbm.at[s])
         if i >= 1:
             reduce_chip(order[i - 1])
-            x_step("y", 1)
-        if last:
-            x_step("c", 1)
         input_partial(s)
     s = order[-1]
-    x_step("c", 1)
     reduce_chip(s)
-    x_step("c", layers)
-    for t in order:
+    c_start(second_unit)
+    for t in range(layers):
         x_ready(layers + t)
+    early = [copy for copy in sent if all(copy is not other for other in second[s])]
+    for copy in early:
+        copy.wait_send()
     for t in order:
         finish(t)
     for copy in out_copies:
         copy.wait()
-    for copy in sent:
+    for copy in second[s]:
         copy.wait_send()
 
 

time: 46.4 us -> 46.3 us (level)
  no operation moved by 1% of the time
where the time goes in v4:
time: 46.3 us; the launch traced here: 46.1 us
  Pallas kernels  44.8 us (97%)
  between operations  0.66 us (1%)
  local copies, waits for them, and re-layouts  0.63 us (1%)
    pallas_call x1, Pallas kernels, per_device(): pl.pallas_call(functools.partial(exchange_kernel, n, layers, rows, width)...  38.2 us
    pallas_call x1, Pallas kernels, per_device(): pl.pallas_call(functools.partial(outer_kernel, tokens ** (-0.5)), in_spec...  6.62 us

profile of v4, /device:TPU:0, one launch (start us, length us, event | category | flops | bytes accessed | tf_op | source)
XLA Modules:
  0.0 46.1 jit_solution(3171459220205173237)
XLA Ops:
  0.6 38.2 %shard_map.68 = (bf16[3,64,1024]{2,1,0:T(8,128)(2,1)}, bf16[3,64,2048]{2,1,0:T(8,128)(2,1)}, bf16[3,4,2048]{2,1,0:T(4,128)(2,1)}) custom-call(bf16[3,4,2048]{2,1,0:T(4,128)(2,1)} %bitcast.6, bf16[3,4,2048]{2,1,0:T(4,128)(2,1)} %bitcast.7, s32[3,64,1024]{2,1,0:T(8,128)} %bitcast.4, bf16[3,2048,1024]{2,1,0:T(8,128)(2,1)} %enc_hbm.1, bf16[6,1024,2048]{2,1,0:T(8,128)(2,1)} %dec_hbm.1), custom_call_target="tpu_custom_call" | custom-call | flops 2415919104 | bytes 37748736 | tf_op jit(solution)/shard_map/pallas_call | solution.py:264
  38.8 0.0 copy-start
  38.8 6.6 %shard_map.69 = bf16[3,2048,1024]{2,1,0:T(8,128)(2,1)} custom-call(bf16[3,64,2048]{2,1,0:T(8,128)(2,1)} %get-tuple-element.5.x_ref, bf16[3,64,1024]{2,1,0:T(8,128)(2,1)} %get-tuple-element.6.pre_ref), custom_call_target="tpu_custom_call" | custom-call | flops 805306368 | bytes 12582912 | tf_op jit(solution)/shard_map/pallas_call | solution.py:318
  45.5 0.0 copy-done
  45.5 0.6 %copy.8 = bf16[4,3,2048]{2,0,1:T(4,128)(2,1)} copy(bf16[4,3,2048]{2,0,1:T(4,128)(2,1)S(1)} %bitcast.5) | data formatting | bytes 98304
Async XLA Ops:
  38.8 6.6 %copy-start = (bf16[3,4,2048]{2,1,0:T(4,128)(2,1)S(1)}, bf16[3,4,2048]{2,1,0:T(4,128)(2,1)}, u32[]{:S(2)}) copy-start(bf16[3,4,2048]{2,1,0:T(4,128)(2,1)} %get-tuple-element.7) | copy-start | bytes 147460

commit v5 on v4

--- a/solution.py
+++ b/solution.py
@@ -152,7 +152,7 @@
             pre_v[s, :, cols] = (total * act_v[s, :, cols].astype(F32)).astype(BF16)
             return carry
 
-        lax.fori_loop(0, local // tile, body, 0)
+        lax.fori_loop(0, local // tile, body, 0, unroll=True)
 
     out_copies = []
 
@@ -173,7 +173,7 @@
                 stage[s, gi, q] = part[gi * 64 : (gi + 1) * 64]
             return carry
 
-        lax.fori_loop(0, 4, body, 0)
+        lax.fori_loop(0, 4, body, 0, unroll=True)
         for gi in range(groups):
             block = stage[s, gi].reshape(256, q_width)
             moved = jnp.dot(perm_t[...], block, preferred_element_type=F32).astype(BF16)

time: 46.3 us -> 44.7 us (0.965)
  Pallas kernels: 44.8 us -> 43.2 us
    pallas_call x1, Pallas kernels: 38.2 us -> 36.6 us  [per_device(): pl.pallas_call(functools.partial(exchange_kernel, n, layers, rows, width)...]
where the time goes in v5:
time: 44.7 us; the launch traced here: 44.5 us
  Pallas kernels  43.2 us (97%)
  between operations  0.66 us (1%)
  local copies, waits for them, and re-layouts  0.63 us (1%)
    pallas_call x1, Pallas kernels, per_device(): pl.pallas_call(functools.partial(exchange_kernel, n, layers, rows, width)...  36.6 us
    pallas_call x1, Pallas kernels, per_device(): pl.pallas_call(functools.partial(outer_kernel, tokens ** (-0.5)), in_spec...  6.63 us

profile of v5, /device:TPU:0, one launch (start us, length us, event | category | flops | bytes accessed | tf_op | source)
XLA Modules:
  0.0 44.5 jit_solution(14483686625908906660)
XLA Ops:
  0.6 36.6 %shard_map.68 = (bf16[3,64,1024]{2,1,0:T(8,128)(2,1)}, bf16[3,64,2048]{2,1,0:T(8,128)(2,1)}, bf16[3,4,2048]{2,1,0:T(4,128)(2,1)}) custom-call(bf16[3,4,2048]{2,1,0:T(4,128)(2,1)} %bitcast.6, bf16[3,4,2048]{2,1,0:T(4,128)(2,1)} %bitcast.7, s32[3,64,1024]{2,1,0:T(8,128)} %bitcast.4, bf16[3,2048,1024]{2,1,0:T(8,128)(2,1)} %enc_hbm.1, bf16[6,1024,2048]{2,1,0:T(8,128)(2,1)} %dec_hbm.1), custom_call_target="tpu_custom_call" | custom-call | flops 2415919104 | bytes 37748736 | tf_op jit(solution)/shard_map/pallas_call | solution.py:264
  37.2 0.0 copy-start
  37.2 6.6 %shard_map.69 = bf16[3,2048,1024]{2,1,0:T(8,128)(2,1)} custom-call(bf16[3,64,2048]{2,1,0:T(8,128)(2,1)} %get-tuple-element.5.x_ref, bf16[3,64,1024]{2,1,0:T(8,128)(2,1)} %get-tuple-element.6.pre_ref), custom_call_target="tpu_custom_call" | custom-call | flops 805306368 | bytes 12582912 | tf_op jit(solution)/shard_map/pallas_call | solution.py:318
  43.9 0.0 copy-done
  43.9 0.6 %copy.8 = bf16[4,3,2048]{2,0,1:T(4,128)(2,1)} copy(bf16[4,3,2048]{2,0,1:T(4,128)(2,1)S(1)} %bitcast.5) | data formatting | bytes 98304
Async XLA Ops:
  37.2 6.6 %copy-start = (bf16[3,4,2048]{2,1,0:T(4,128)(2,1)S(1)}, bf16[3,4,2048]{2,1,0:T(4,128)(2,1)}, u32[]{:S(2)}) copy-start(bf16[3,4,2048]{2,1,0:T(4,128)(2,1)} %get-tuple-element.7) | copy-start | bytes 147460
